TPU v7x, 32 devices: a whole 2x2x4 slice. The times are simulated.
32 devices in a mesh: blk: 8 (over z, core), fsdp: 4 (over y, x).
Axes of the slice: x: 2, y: 2, z: 4, core: 2. Of those that a mesh axis runs over, the one named last changes fastest.
Arguments:
- context: bfloat16 [8, 512, 2048], P('blk', 'fsdp'), may hold values from -6 to 6
- hidden: bfloat16 [8, 512, 4096], P('blk', 'fsdp'), may hold values from -6 to 6
- cotangent: bfloat16 [8, 512, 4096], P('blk', 'fsdp'), may hold values from -6 to 6
- gain: float32 [8, 4096], P('blk'), may hold values from 0.3 to 3
- weight: bfloat16 [8, 2048, 4096], P('blk', None, 'fsdp'), may hold values from -6 to 6
- step_counts: int32 [8], P('blk'), may hold values from 1 to 256
Outputs:
- new_weight: bfloat16 [8, 2048, 4096], P('blk', None, 'fsdp')
All inputs are finite; a program needn't handle non-finite values.
Results may differ from a plain program's by a relative error of at most 0.0038.
Values may be sent and summed in bfloat16 or wider, within the bound.
A program may use at most 64 MiB of HBM per device.

v0:
```python
import math

import jax
import jax.numpy as jnp
from jax import lax
from jax.sharding import PartitionSpec as P


def passed_along(block, axis, distance):
    devices = range(lax.axis_size(axis))
    route = [((i - distance) % len(devices), i) for i in devices]
    return lax.ppermute(block, axis, route)


def body(context, hidden, cotangent, gain, weight, step_counts):
    inputs = context[0]
    own = weight[0]
    width = inputs.shape[1]
    group = lax.axis_size("fsdp")
    rows = inputs.shape[0] * group
    scale = 1.0 / math.sqrt(width)
    rate = 0.5 * math.sqrt(width / rows)
    counts_wire = step_counts.astype(jnp.bfloat16)
    low_weight, low_count = passed_along((weight, counts_wire), "blk", 1)
    high_weight, high_count = passed_along((weight, counts_wire), "blk", -1)
    gathered = lax.all_gather(inputs, "fsdp", axis=0, tiled=True)
    branch = (jnp.dot(gathered, own, preferred_element_type=jnp.float32) * scale).astype(
        jnp.bfloat16
    )
    branch_rows = lax.all_to_all(branch, "fsdp", split_axis=0, concat_axis=1, tiled=True)
    residual_out = hidden[0].astype(jnp.float32) + branch_rows.astype(jnp.float32)
    inv_rms = lax.rsqrt(jnp.mean(residual_out * residual_out, axis=-1, keepdims=True) + 1e-05)
    scaled = gain[0][None, :] * cotangent[0].astype(jnp.float32)
    cross = jnp.mean(scaled * residual_out, axis=-1, keepdims=True)
    grad_rows = (inv_rms * scaled - residual_out * inv_rms**3 * cross).astype(jnp.bfloat16)
    out_grad = lax.all_to_all(grad_rows, "fsdp", split_axis=1, concat_axis=0, tiled=True)
    grad = (
        lax.dot_general(
            gathered, out_grad, (((0,), (0,)), ((), ())), preferred_element_type=jnp.float32
        )
        * scale
    )
    lower_c = low_count.astype(jnp.float32)[0]
    own_c = step_counts.astype(jnp.float32)[0]
    upper_c = high_count.astype(jnp.float32)[0]
    total = lower_c + own_c + upper_c
    mixed = (
        lower_c * low_weight[0].astype(jnp.float32)
        + own_c * own.astype(jnp.float32)
        + upper_c * high_weight[0].astype(jnp.float32)
    ) / total
    return (mixed - rate * grad).astype(jnp.bfloat16)[None]


def solution(mesh):
    return jax.shard_map(
        body,
        mesh=mesh,
        in_specs=(
            P("blk", "fsdp", None),
            P("blk", "fsdp", None),
            P("blk", "fsdp", None),
            P("blk", None),
            P("blk", None, "fsdp"),
            P("blk"),
        ),
        out_specs=P("blk", None, "fsdp"),
        check_vma=False,
    )
```

profile of v0, /device:TPU:0, one launch (start us, length us, event | category | flops | bytes accessed | tf_op | source)
XLA Modules:
  0.0 136.4 jit_solution(17001051425902305718)
XLA Ops:
  6.5 0.7 all-gather.3.cloned.1.call-update
  7.3 6.4 %copy.7 = bf16[1,2048,1024]{1,2,0:T(8,128)(2,1)} copy(bf16[1,2048,1024]{2,1,0:T(8,128)(2,1)} %param.10) | data formatting | bytes 8388608 | tf_op args[4]
  13.7 4.5 %collective-permute-start.3 = (bf16[1,2048,1024]{1,2,0:T(8,128)(2,1)}, bf16[1,2048,1024]{1,2,0:T(8,128)(2,1)}, u32[]{:S(2)}, u32[]{:S(2)}) collective-permute-start(bf16[1,2048,1024]{1,2,0:T(8,128)(2,1)} %copy.7), channel_id=1, source_target_pairs={{4,0},{8,4},{12,8},{16,12},{20,16},{24,20},{28,24},{0,28},{5,1},{9... | collective-permute-start | bytes 12582920 | tf_op jit(solution)/shard_map/ppermute | solution.py:12
  18.2 29.1 %all-gather.3.cloned.1.call-done = bf16[1,512,2048]{2,1,0:T(8,128)(2,1)} async-done(((bf16[1,128,2048]{2,1,0:T(8,128)(2,1)}), bf16[1,512,2048]{2,1,0:T(8,128)(2,1)}) %all-gather.3.cloned.1.call-update) | async-done | bytes 2097168 | tf_op jit(solution)/shard_map/all_gather | solution.py:26
  47.2 6.2 %multiply_convert_fusion = bf16[512,1024]{1,0:T(8,128)(2,1)} fusion(bf16[1,2048,1024]{2,1,0:T(8,128)(2,1)} %param.10, bf16[1,512,2048]{2,1,0:T(8,128)(2,1)} %all-gather.3.cloned.1.call-done), kind=kOutput, calls=%fused_computation.25 | convolution fusion | flops 2148532224 | bytes 7340032 | tf_op jit(solution)/shard_map/dot_general | solution.py:27
  53.4 3.6 %all-to-all-start = ((bf16[4,128,1024]{2,1,0:T(8,128)(2,1)}), bf16[4,128,1024]{2,1,0:T(8,128)(2,1)S(1)}, u32[]{:S(2)}, u32[]{:S(2)}) async-start(bf16[4,128,1024]{2,1,0:T(8,128)(2,1)} %bitcast.10), calls=%async_computation | async-start | bytes 2097152 | tf_op jit(solution)/shard_map/all_to_all | solution.py:30
  57.1 0.5 broadcast.54
  57.6 0.6 reduce.3
  58.2 2.7 %reshape.67 = f32[128,4,1024]{2,1,0:T(4,128)S(1)} reshape(bf16[1,128,4096]{2,1,0:T(8,128)(2,1)} %param.7) | data formatting | bytes 3145728 | tf_op jit(solution)/shard_map/convert_element_type | solution.py:31
  61.0 3.7 %reshape.66 = f32[128,4,1024]{2,1,0:T(4,128)} reshape(bf16[1,128,4096]{2,1,0:T(8,128)(2,1)} %param.8) | data formatting | bytes 3145728 | tf_op jit(solution)/shard_map/convert_element_type | solution.py:33
  64.7 6.3 %all-to-all-done = bf16[4,128,1024]{2,1,0:T(8,128)(2,1)S(1)} async-done(((bf16[4,128,1024]{2,1,0:T(8,128)(2,1)}), bf16[4,128,1024]{2,1,0:T(8,128)(2,1)S(1)}, u32[]{:S(2)}, u32[]{:S(2)}) %all-to-all-start) | async-done | bytes 1048608 | tf_op jit(solution)/shard_map/all_to_all | solution.py:30
  71.0 0.2 convert_bitcast_fusion
  71.2 0.2 copy.14
  71.5 1.0 copy-done.1
  72.5 0.3 copy-done.2
  72.8 0.7 multiply_reduce_fusion
  73.5 0.9 copy-done
  74.4 3.8 %fusion.9 = bf16[128,4,1024]{2,0,1:T(8,128)(2,1)} fusion(bf16[4,128,1024]{2,1,0:T(8,128)(2,1)S(1)} %all-to-all-done, f32[128,4,1024]{2,1,0:T(4,128)S(1)} %reshape.67, f32[128,4,1024]{2,1,0:T(4,128)S(1)} %copy-done, f32[128]{0:T(128)S(1)} %get-tuple-element.9, f32[128]{0:T(128)S(1)} %get-tuple-element.8, f32[4,1024]{1,0:T(4,128)S(1)} %mul.101, ...), kind=kLoop, calls=%fused_computation.14 | loop fusion | flops 4194304 | bytes 6309376 | tf_op jit(solution)/shard_map/convert_element_type | solution.py:35
  78.1 3.6 %all-to-all-start.1 = ((bf16[128,4,1024]{2,0,1:T(8,128)(2,1)}), bf16[128,4,1024]{2,0,1:T(8,128)(2,1)S(1)}, u32[]{:S(2)}, u32[]{:S(2)}) async-start(bf16[128,4,1024]{2,0,1:T(8,128)(2,1)} %fusion.9), calls=%async_computation.1 | async-start | bytes 2097152 | tf_op jit(solution)/shard_map/all_to_all | solution.py:36
  82.4 25.0 %collective-permute-start.2 = (bf16[1]{0:T(256)(128)(2,1)}, bf16[1]{0:T(256)(128)(2,1)}, u32[]{:S(2)}, u32[]{:S(2)}) collective-permute-start(bf16[1]{0:T(256)(128)(2,1)} %convert_element_type.66), channel_id=1, source_target_pairs={{4,0},{8,4},{12,8},{16,12},{20,16},{24,20},{28,24},{0,28},{5,1},{9... | collective-permute-start | bytes 14 | tf_op jit(solution)/shard_map/ppermute | solution.py:12
  107.5 0.8 collective-permute-start
  108.9 3.3 %collective-permute-done = bf16[1]{0:T(256)(128)(2,1)} collective-permute-done((bf16[1]{0:T(256)(128)(2,1)}, bf16[1]{0:T(256)(128)(2,1)}, u32[]{:S(2)}, u32[]{:S(2)}) %collective-permute-start) | collective-permute-done | bytes 34 | tf_op jit(solution)/shard_map/ppermute | solution.py:12
  114.2 9.0 %fusion.4 = bf16[1,2048,1024]{1,2,0:T(8,128)(2,1)} fusion(f32[]{:T(128)S(6)} %add.35, bf16[1,2048,1024]{1,2,0:T(8,128)(2,1)} %collective-permute-done.3, f32[]{:T(128)S(6)} %convert.10, bf16[1,2048,1024]{1,2,0:T(8,128)(2,1)} %copy.7, f32[]{:T(128)} %bitcast.2, bf16[1,2048,1024]{1,2,0:T(8,128)(2,1)} %collective-permute-done.1, f32[]{:T(128)S(6)} %convert.9, ...), kind=kOutput, calls=%fused_computation.7 | convolution fusion | flops 2172649472 | bytes 19922960 | tf_op jit(solution)/shard_map/dot_general | solution.py:38
  123.2 6.4 %copy.13 = bf16[1,2048,1024]{2,1,0:T(8,128)(2,1)} copy(bf16[1,2048,1024]{1,2,0:T(8,128)(2,1)} %fusion.4) | data formatting | bytes 8388608 | tf_op jit(solution)/shard_map/broadcast_in_dim | solution.py:52
  (15 shorter events, 0.1 us)
Async XLA Ops:
  6.5 40.7 %all-gather.3.cloned.1.call-start = ((), (), s32[]{:S(2)}) async-start(), calls=%async_computation.2 | async-start | bytes 2621440 | tf_op jit(solution)/shard_map/all_gather | solution.py:26
  13.7 100.5 %collective-permute-start.3 = (bf16[1,2048,1024]{1,2,0:T(8,128)(2,1)}, bf16[1,2048,1024]{1,2,0:T(8,128)(2,1)}, u32[]{:S(2)}, u32[]{:S(2)}) collective-permute-start(bf16[1,2048,1024]{1,2,0:T(8,128)(2,1)} %copy.7), channel_id=1, source_target_pairs={{4,0},{8,4},{12,8},{16,12},{20,16},{24,20},{28,24},{0,28},{5,1},{9... | collective-permute-start | bytes 12582920 | tf_op jit(solution)/shard_map/ppermute | solution.py:12
  18.2 96.0 %collective-permute-start.1 = (bf16[1,2048,1024]{1,2,0:T(8,128)(2,1)}, bf16[1,2048,1024]{1,2,0:T(8,128)(2,1)}, u32[]{:S(2)}, u32[]{:S(2)}) collective-permute-start(bf16[1,2048,1024]{1,2,0:T(8,128)(2,1)} %copy.7), channel_id=1, source_target_pairs={{28,0},{0,4},{4,8},{8,12},{12,16},{16,20},{20,24},{24,28},{29,1},{... | collective-permute-start | bytes 12582920 | tf_op jit(solution)/shard_map/ppermute | solution.py:12
  53.4 4.1 %copy-start.3 = (f32[1,4096]{1,0:T(1,128)S(1)}, f32[1,4096]{1,0:T(1,128)}, u32[]{:S(2)}) copy-start(f32[1,4096]{1,0:T(1,128)} %param.9) | copy-start | bytes 49156
  53.4 17.5 %all-to-all-start = ((bf16[4,128,1024]{2,1,0:T(8,128)(2,1)}), bf16[4,128,1024]{2,1,0:T(8,128)(2,1)S(1)}, u32[]{:S(2)}, u32[]{:S(2)}) async-start(bf16[4,128,1024]{2,1,0:T(8,128)(2,1)} %bitcast.10), calls=%async_computation | async-start | bytes 2097152 | tf_op jit(solution)/shard_map/all_to_all | solution.py:30
  71.2 1.2 copy-start.1
  71.2 1.5 %copy-start.2 = (bf16[1,128,4096]{2,1,0:T(8,128)(2,1)S(1)}, bf16[1,128,4096]{2,1,0:T(8,128)(2,1)}, u32[]{:S(2)}) copy-start(bf16[1,128,4096]{2,1,0:T(8,128)(2,1)} %param.8) | copy-start | bytes 3145732
  72.8 1.6 %copy-start = (f32[128,4,1024]{2,1,0:T(4,128)S(1)}, f32[128,4,1024]{2,1,0:T(4,128)}, u32[]{:S(2)}) copy-start(f32[128,4,1024]{2,1,0:T(4,128)} %reshape.66) | copy-start | bytes 6291460
  78.1 36.1 %copy-start.4 = (bf16[1,512,2048]{2,1,0:T(8,128)(2,1)S(1)}, bf16[1,512,2048]{2,1,0:T(8,128)(2,1)}, u32[]{:S(2)}) copy-start(bf16[1,512,2048]{2,1,0:T(8,128)(2,1)} %all-gather.3.cloned.1.call-done) | copy-start | bytes 6291460
  78.1 36.0 %all-to-all-start.1 = ((bf16[128,4,1024]{2,0,1:T(8,128)(2,1)}), bf16[128,4,1024]{2,0,1:T(8,128)(2,1)S(1)}, u32[]{:S(2)}, u32[]{:S(2)}) async-start(bf16[128,4,1024]{2,0,1:T(8,128)(2,1)} %fusion.9), calls=%async_computation.1 | async-start | bytes 2097152 | tf_op jit(solution)/shard_map/all_to_all | solution.py:36
  82.4 25.9 %collective-permute-start.2 = (bf16[1]{0:T(256)(128)(2,1)}, bf16[1]{0:T(256)(128)(2,1)}, u32[]{:S(2)}, u32[]{:S(2)}) collective-permute-start(bf16[1]{0:T(256)(128)(2,1)} %convert_element_type.66), channel_id=1, source_target_pairs={{4,0},{8,4},{12,8},{16,12},{20,16},{24,20},{28,24},{0,28},{5,1},{9... | collective-permute-start | bytes 14 | tf_op jit(solution)/shard_map/ppermute | solution.py:12
  107.5 4.7 %collective-permute-start = (bf16[1]{0:T(256)(128)(2,1)}, bf16[1]{0:T(256)(128)(2,1)}, u32[]{:S(2)}, u32[]{:S(2)}) collective-permute-start(bf16[1]{0:T(256)(128)(2,1)} %convert_element_type.66), channel_id=1, source_target_pairs={{28,0},{0,4},{4,8},{8,12},{12,16},{16,20},{20,24},{24,28},{29,1},{... | collective-permute-start | bytes 14 | tf_op jit(solution)/shard_map/ppermute | solution.py:12
Sparse Core Ops, SparseCore 0:
  9.2 38.0 all-gather.2
where the time goes:
time: 137 us; the launch traced here: 136 us
  waiting for transfers between devices  39.4 us (29%)
  starting transfers between devices  37.6 us (27%)
  local copies, waits for them, and re-layouts  22.2 us (16%)
  between operations  16.7 us (12%)
  matrix products  15.2 us (11%)
  other arithmetic  5.3 us (4%)
    ppermute x4, starting transfers between devices, passed_along(): return lax.ppermute(block, axis, route)  30.3 us
    all_gather x1, waiting for transfers between devices, body(): gathered = lax.all_gather(inputs, 'fsdp', axis=0, tiled=True)  29.1 us
    unnamed x12, local copies, waits for them, and re-layouts  9.12 us
    dot_general x1, matrix products, body(): lax.dot_general(gathered, out_grad, (((0,), (0,)), ((), ())), preferred_e...  8.97 us
    broadcast_in_dim x1, local copies, waits for them, and re-layouts, body(): return (mixed - rate * grad).astype(jnp.bfloat16)[None]  6.39 us
    all_to_all x1, waiting for transfers between devices, body(): lax.all_to_all(branch, 'fsdp', split_axis=0, concat_axis=1, tiled=True)  6.27 us
    dot_general x1, matrix products, body(): jnp.dot(gathered, own, preferred_element_type=jnp.float32) * scale  6.19 us
    convert_element_type x1, other arithmetic, body(): (inv_rms * scaled - residual_out * inv_rms ** 3 * cross).astype(jnp.bfloa...  3.78 us
  transfers between devices with their start and end apart: 7, of which 3 were waited for; matrix products, arithmetic and copies ran while one was open for 18% of the time, Pallas kernels for 0%

commit v1 on v0

v1 whole, which is shorter than its diff:
```python
import functools
import math

import jax
import jax.numpy as jnp
from jax import lax
from jax.experimental import pallas as pl
from jax.experimental.pallas import tpu as pltpu
from jax.sharding import PartitionSpec as P

MESH = pl.DeviceIdType.MESH
CHUNKS = 16
DEPTH = 256
ROWS = 16
COLS = 256


def kernel(
    blocks,
    group,
    context,
    hidden,
    cotangent,
    gain,
    weight,
    count,
    out,
    low,
    high,
    own,
    acc,
    stage,
    tokens,
    branch_out,
    branch_in,
    grad_out,
    grad_in,
    hid,
    cot,
    gains,
    counts,
    w_send,
    w_recv,
    x_send,
    x_recv,
    b_send,
    b_recv,
    g_send,
    g_recv,
    c_send,
    c_recv,
    l_sem,
    o_sem,
):
    rank = lax.axis_index("blk")
    me = lax.axis_index("fsdp")
    up = lax.rem(rank + 1, blocks)
    down = lax.rem(rank + blocks - 1, blocks)
    per, width = context.shape
    part = weight.shape[1]
    model = part * group
    scale = 1.0 / math.sqrt(width)
    rate = 0.5 * math.sqrt(width / (per * group))
    piece = width // CHUNKS

    def peer(i):
        return lax.rem(me + i, group)

    def rows_of(p):
        return pl.ds(pl.multiple_of(p * per, per), per)

    barrier = pltpu.get_barrier_semaphore()
    for other in (up, down):
        pl.semaphore_signal(barrier, inc=1, device_id=(other, me), device_id_type=MESH)
    for i in range(1, group):
        pl.semaphore_signal(barrier, inc=1, device_id=(rank, peer(i)), device_id_type=MESH)
    pl.semaphore_wait(barrier, group + 1)

    def weight_copy(way, c):
        rows = pl.ds(c * piece, piece)
        other, landing = ((up, low), (down, high))[way]
        return pltpu.make_async_remote_copy(
            src_ref=weight.at[rows],
            dst_ref=landing.at[rows],
            send_sem=w_send.at[way, c],
            recv_sem=w_recv.at[way, c],
            device_id=(other, me),
            device_id_type=MESH,
        )

    def token_copy(source, slot, target):
        return pltpu.make_async_remote_copy(
            src_ref=source,
            dst_ref=tokens.at[rows_of(slot)],
            send_sem=x_send.at[target],
            recv_sem=x_recv.at[slot],
            device_id=(rank, target),
            device_id_type=MESH,
        )

    def branch_copy(slot, target):
        return pltpu.make_async_remote_copy(
            src_ref=branch_out.at[rows_of(target)],
            dst_ref=branch_in.at[rows_of(slot)],
            send_sem=b_send.at[target],
            recv_sem=b_recv.at[slot],
            device_id=(rank, target),
            device_id_type=MESH,
        )

    def grad_copy(slot, target):
        return pltpu.make_async_remote_copy(
            src_ref=grad_out.at[rows_of(target)],
            dst_ref=grad_in.at[rows_of(slot)],
            send_sem=g_send.at[target],
            recv_sem=g_recv.at[slot],
            device_id=(rank, target),
            device_id_type=MESH,
        )

    def count_copy(way):
        other = (up, down)[way]
        return pltpu.make_async_remote_copy(
            src_ref=counts.at[0],
            dst_ref=counts.at[1 + way],
            send_sem=c_send.at[way],
            recv_sem=c_recv.at[way],
            device_id=(other, me),
            device_id_type=MESH,
        )

    for c in range(CHUNKS):
        for way in range(2):
            weight_copy(way, c).start()
    for i in range(1, group):
        token_copy(context, me, peer(i)).start()

    loads = [
        pltpu.make_async_copy(context, tokens.at[rows_of(me)], l_sem.at[0]),
        pltpu.make_async_copy(weight, own, l_sem.at[1]),
        pltpu.make_async_copy(hidden, hid, l_sem.at[2]),
        pltpu.make_async_copy(cotangent, cot, l_sem.at[3]),
        pltpu.make_async_copy(gain, gains, l_sem.at[4]),
    ]
    for load in loads:
        load.start()

    counts[0] = jnp.full(counts.shape[1:], count[0], jnp.int32)
    for way in range(2):
        count_copy(way).start()

    loads[0].wait()
    loads[1].wait()

    def make_branch(p, target):
        block = tokens[rows_of(p)]

        @pl.loop(0, part // COLS)
        def _(n):
            columns = pl.ds(pl.multiple_of(n * COLS, COLS), COLS)
            dot = jnp.dot(block, own[:, columns], preferred_element_type=jnp.float32)
            target[rows_of(p), columns] = (dot * scale).astype(jnp.bfloat16)

    make_branch(me, branch_in)
    for i in range(1, group):
        p = peer(i)
        token_copy(context, p, p).wait_recv()
        make_branch(p, branch_out)
        branch_copy(me, p).start()

    for load in loads[2:]:
        load.wait()
    for i in range(1, group):
        p = peer(i)
        branch_copy(p, p).wait_recv()

    @pl.loop(0, per // ROWS)
    def _(t):
        rows = pl.ds(pl.multiple_of(t * ROWS, ROWS), ROWS)

        def terms(s):
            columns = pl.ds(s * part, part)
            slot = pl.ds(pl.multiple_of(s * per + t * ROWS, ROWS), ROWS)
            residual = hid[rows, columns].astype(jnp.float32) + branch_in[slot, :].astype(
                jnp.float32
            )
            scaled = gains[:, columns] * cot[rows, columns].astype(jnp.float32)
            return slot, residual, scaled

        squares = jnp.zeros((ROWS, 1), jnp.float32)
        cross = jnp.zeros((ROWS, 1), jnp.float32)
        for s in range(group):
            _, residual, scaled = terms(s)
            squares += jnp.sum(residual * residual, axis=-1, keepdims=True)
            cross += jnp.sum(scaled * residual, axis=-1, keepdims=True)
        inv_rms = lax.rsqrt(squares / model + 1e-05)
        factor = inv_rms * inv_rms * inv_rms * (cross / model)
        for s in range(group):
            slot, residual, scaled = terms(s)
            grad_out[slot, :] = (inv_rms * scaled - residual * factor).astype(jnp.bfloat16)

    for i in range(1, group):
        grad_copy(me, peer(i)).start()
    mine = pltpu.make_async_copy(grad_out.at[rows_of(me)], grad_in.at[rows_of(me)], l_sem.at[5])
    mine.start()

    for way in range(2):
        count_copy(way).wait_recv()
    own_c = counts[0][0:1, 0:1].astype(jnp.float32)
    low_c = counts[1][0:1, 0:1].astype(jnp.float32)
    high_c = counts[2][0:1, 0:1].astype(jnp.float32)
    total = low_c + own_c + high_c
    own_c, low_c, high_c = own_c / total, low_c / total, high_c / total

    mine.wait()
    for i in range(1, group):
        p = peer(i)
        grad_copy(p, p).wait_recv()

    @pl.loop(0, width // DEPTH)
    def _(k):
        rows = pl.ds(pl.multiple_of(k * DEPTH, DEPTH), DEPTH)
        grad = lax.dot_general(
            tokens[:, rows],
            grad_in[...],
            (((0,), (0,)), ((), ())),
            preferred_element_type=jnp.float32,
        )
        acc[rows, :] = own_c * own[rows, :].astype(jnp.float32) - (rate * scale) * grad

    def result(c):
        rows = pl.ds(c * piece, piece)
        return pltpu.make_async_copy(stage.at[rows], out.at[rows], o_sem.at[c])

    for c in range(CHUNKS):
        rows = pl.ds(c * piece, piece)
        for way in range(2):
            weight_copy(way, c).wait_recv()
        stage[rows, :] = (
            acc[rows, :]
            + low_c * low[rows, :].astype(jnp.float32)
            + high_c * high[rows, :].astype(jnp.float32)
        ).astype(jnp.bfloat16)
        result(c).start()

    for i in range(1, group):
        p = peer(i)
        token_copy(context, me, p).wait_send()
        branch_copy(me, p).wait_send()
        grad_copy(me, p).wait_send()
    for way in range(2):
        count_copy(way).wait_send()
        for c in range(CHUNKS):
            weight_copy(way, c).wait_send()
    for c in range(CHUNKS):
        result(c).wait()


def body(context, hidden, cotangent, gain, weight, step_counts):
    blocks = lax.axis_size("blk")
    group = lax.axis_size("fsdp")
    _, per, width = context.shape
    part = weight.shape[2]
    half = jnp.bfloat16
    flops = 4 * per * group * width * part
    hbm = pl.BlockSpec(memory_space=pl.ANY)
    new = pl.pallas_call(
        functools.partial(kernel, blocks, group),
        out_shape=jax.ShapeDtypeStruct((width, part), half),
        in_specs=[hbm] * 5 + [pl.BlockSpec(memory_space=pltpu.SMEM)],
        out_specs=hbm,
        scratch_shapes=[
            pltpu.VMEM((width, part), half),
            pltpu.VMEM((width, part), half),
            pltpu.VMEM((width, part), half),
            pltpu.VMEM((width, part), jnp.float32),
            pltpu.VMEM((width, part), half),
            pltpu.VMEM((per * group, width), half),
            pltpu.VMEM((per * group, part), half),
            pltpu.VMEM((per * group, part), half),
            pltpu.VMEM((per * group, part), half),
            pltpu.VMEM((per * group, part), half),
            pltpu.VMEM((per, part * group), half),
            pltpu.VMEM((per, part * group), half),
            pltpu.VMEM((1, part * group), jnp.float32),
            pltpu.VMEM((3, 8, 128), jnp.int32),
            pltpu.SemaphoreType.DMA((2, CHUNKS)),
            pltpu.SemaphoreType.DMA((2, CHUNKS)),
            pltpu.SemaphoreType.DMA((group,)),
            pltpu.SemaphoreType.DMA((group,)),
            pltpu.SemaphoreType.DMA((group,)),
            pltpu.SemaphoreType.DMA((group,)),
            pltpu.SemaphoreType.DMA((group,)),
            pltpu.SemaphoreType.DMA((group,)),
            pltpu.SemaphoreType.DMA((2,)),
            pltpu.SemaphoreType.DMA((2,)),
            pltpu.SemaphoreType.DMA((6,)),
            pltpu.SemaphoreType.DMA((CHUNKS,)),
        ],
        compiler_params=pltpu.CompilerParams(
            collective_id=1, has_side_effects=True, vmem_limit_bytes=54 * 2**20
        ),
        cost_estimate=pl.CostEstimate(
            flops=flops, bytes_accessed=24 * 2**20, transcendentals=0
        ),
    )(context[0], hidden[0], cotangent[0], gain, weight[0], step_counts)
    return new[None]


def solution(mesh):
    return jax.shard_map(
        body,
        mesh=mesh,
        in_specs=(
            P("blk", "fsdp", None),
            P("blk", "fsdp", None),
            P("blk", "fsdp", None),
            P("blk", None),
            P("blk", None, "fsdp"),
            P("blk"),
        ),
        out_specs=P("blk", None, "fsdp"),
        check_vma=False,
    )
```

time: 137 us -> 110 us (0.80)
  Pallas kernels: 0 us -> 105 us
  waiting for transfers between devices: 39.4 us -> 0 us
  starting transfers between devices: 37.6 us -> 0 us
  local copies, waits for them, and re-layouts: 22.2 us -> 4.64 us
  between operations: 16.7 us -> 0.66 us
  matrix products: 15.2 us -> 0 us
  other arithmetic: 5.3 us -> 0 us
    pallas_call x0 -> x1, Pallas kernels: none -> 105 us  [body(): pl.pallas_call(functools.partial(kernel, blocks, group), out_shape=jax.Sh...]
    ppermute x4 -> x0, starting transfers between devices: 30.3 us -> none  [passed_along(): return lax.ppermute(block, axis, route)]
    all_gather x1 -> x0, waiting for transfers between devices: 29.1 us -> none  [body(): gathered = lax.all_gather(inputs, 'fsdp', axis=0, tiled=True)]
    dot_general x2 -> x0, matrix products: 15.2 us -> none  [the longest x1 8.97 us: body(): lax.dot_general(gathered, out_grad, (((0,), (0,)), ((), ())), preferred_e...]
    all_to_all x2 -> x0, starting transfers between devices: 7.29 us -> none  [the longest x1 3.65 us: body(): lax.all_to_all(branch, 'fsdp', split_axis=0, concat_axis=1, tiled=True)]
    convert_element_type x3 -> x0, local copies, waits for them, and re-layouts: 6.72 us -> none  [the longest x1 3.74 us: body(): scaled = gain[0][None, :] * cotangent[0].astype(jnp.float32)]
    broadcast_in_dim x1 -> x0, local copies, waits for them, and re-layouts: 6.39 us -> none  [body(): return (mixed - rate * grad).astype(jnp.bfloat16)[None]]
    all_to_all x2 -> x0, waiting for transfers between devices: 6.27 us -> none  [the longest x1 6.27 us: body(): lax.all_to_all(branch, 'fsdp', split_axis=0, concat_axis=1, tiled=True)]
  transfers between devices with their start and end apart: 7 -> 0, of which waited for: 3 -> 0; matrix products, arithmetic and copies ran while one was open for 18% -> 0% of each run, Pallas kernels for 0% -> 0%
where the time goes in v1:
time: 110 us
  Pallas kernels  105 us (95%)
  local copies, waits for them, and re-layouts  4.64 us (4%)
    pallas_call x1, Pallas kernels, body(): pl.pallas_call(functools.partial(kernel, blocks, group), out_shape=jax.Sh...  105 us
    unnamed x1, local copies, waits for them, and re-layouts  4.64 us

profile of v1, /device:TPU:0, one launch (start us, length us, event | category | flops | bytes accessed | tf_op | source)
XLA Modules:
  0.0 109.9 jit_solution(16547571630540120629)
XLA Ops:
  0.7 104.6 %shard_map.64 = bf16[2048,1024]{1,0:T(8,128)(2,1)} custom-call(bf16[128,2048]{1,0:T(8,128)(2,1)} %bitcast.9, bf16[128,4096]{1,0:T(8,128)(2,1)} %bitcast.7, bf16[128,4096]{1,0:T(8,128)(2,1)} %bitcast.8, f32[1,4096]{1,0:T(1,128)} %gain.1, bf16[2048,1024]{1,0:T(8,128)(2,1)} %bitcast.6, s32[1]{0:T(128)S(6)} %copy.8.count), custom_call_target="tpu_custom_call" | custom-call | flops 4294967296 | bytes 25165824 | tf_op jit(solution)/shard_map/pallas_call | solution.py:267
  105.2 4.6 %copy.9 = bf16[1,2048,1024]{2,1,0:T(8,128)(2,1)} copy(bf16[1,2048,1024]{2,1,0:T(8,128)(2,1)} %bitcast.5) | data formatting | bytes 8388608

commit v2 on v1

--- a/solution.py
+++ b/solution.py
@@ -129,6 +129,10 @@
             device_id_type=MESH,
         )
 
+    counts[0] = jnp.full(counts.shape[1:], count[0], jnp.int32)
+    for way in range(2):
+        count_copy(way).start()
+
     for c in range(CHUNKS):
         for way in range(2):
             weight_copy(way, c).start()
@@ -144,10 +148,6 @@
     ]
     for load in loads:
         load.start()
-
-    counts[0] = jnp.full(counts.shape[1:], count[0], jnp.int32)
-    for way in range(2):
-        count_copy(way).start()
 
     loads[0].wait()
     loads[1].wait()
@@ -263,12 +263,12 @@
     part = weight.shape[2]
     half = jnp.bfloat16
     flops = 4 * per * group * width * part
-    hbm = pl.BlockSpec(memory_space=pl.ANY)
+    hbm = pl.BlockSpec(memory_space=pltpu.HBM)
     new = pl.pallas_call(
         functools.partial(kernel, blocks, group),
         out_shape=jax.ShapeDtypeStruct((width, part), half),
         in_specs=[hbm] * 5 + [pl.BlockSpec(memory_space=pltpu.SMEM)],
-        out_specs=hbm,
+        out_specs=pl.BlockSpec(memory_space=pl.ANY),
         scratch_shapes=[
             pltpu.VMEM((width, part), half),
             pltpu.VMEM((width, part), half),
@@ -298,12 +298,18 @@
             pltpu.SemaphoreType.DMA((CHUNKS,)),
         ],
         compiler_params=pltpu.CompilerParams(
-            collective_id=1, has_side_effects=True, vmem_limit_bytes=54 * 2**20
+            collective_id=1, has_side_effects=True, vmem_limit_bytes=46 * 2**20
         ),
         cost_estimate=pl.CostEstimate(
             flops=flops, bytes_accessed=24 * 2**20, transcendentals=0
         ),
-    )(context[0], hidden[0], cotangent[0], gain, weight[0], step_counts)
+    )(
+        *(
+            pltpu.with_memory_space_constraint(x, pltpu.HBM)
+            for x in (context[0], hidden[0], cotangent[0], gain, weight[0])
+        ),
+        step_counts,
+    )
     return new[None]
 
 

time: 110 us -> 101 us (0.918)
  Pallas kernels: 105 us -> 98.2 us
  local copies, waits for them, and re-layouts: 4.64 us -> 2.02 us
    pallas_call x1, Pallas kernels: 105 us -> 98.2 us  [body(): pl.pallas_call(functools.partial(kernel, blocks, group), out_shape=jax.Sh...]
    unnamed x1, local copies, waits for them, and re-layouts: 4.64 us -> 2.02 us
where the time goes in v2:
time: 101 us
  Pallas kernels  98.2 us (97%)
  local copies, waits for them, and re-layouts  2.02 us (2%)
    pallas_call x1, Pallas kernels, body(): pl.pallas_call(functools.partial(kernel, blocks, group), out_shape=jax.Sh...  98.2 us

profile of v2, /device:TPU:0, one launch (start us, length us, event | category | flops | bytes accessed | tf_op | source)
XLA Modules:
  0.0 100.9 jit_solution(11460214710527139841)
XLA Ops:
  0.7 98.2 %shard_map.64 = bf16[2048,1024]{1,0:T(8,128)(2,1)S(1)} custom-call(bf16[128,2048]{1,0:T(8,128)(2,1)} %bitcast.9, bf16[128,4096]{1,0:T(8,128)(2,1)} %bitcast.7, bf16[128,4096]{1,0:T(8,128)(2,1)} %bitcast.8, f32[1,4096]{1,0:T(1,128)} %gain.1, bf16[2048,1024]{1,0:T(8,128)(2,1)} %bitcast.6, s32[1]{0:T(128)S(6)} %copy.8.count), custom_call_target="tpu_custom_call" | custom-call | flops 4294967296 | bytes 25165824 | tf_op jit(solution)/shard_map/pallas_call | solution.py:267
  98.9 2.0 %copy.9 = bf16[1,2048,1024]{2,1,0:T(8,128)(2,1)} copy(bf16[1,2048,1024]{2,1,0:T(8,128)(2,1)S(1)} %bitcast.5) | data formatting | bytes 8388608

commit v3 on v2

--- a/solution.py
+++ b/solution.py
@@ -9,7 +9,8 @@
 from jax.sharding import PartitionSpec as P
 
 MESH = pl.DeviceIdType.MESH
-CHUNKS = 16
+CUTS = (0, 8, 16, 24, 32, 40, 48, 56, 60, 62, 64)
+CHUNKS = len(CUTS) - 1
 DEPTH = 256
 ROWS = 16
 COLS = 256
@@ -29,7 +30,6 @@
     high,
     own,
     acc,
-    stage,
     tokens,
     branch_out,
     branch_in,
@@ -50,7 +50,6 @@
     c_send,
     c_recv,
     l_sem,
-    o_sem,
 ):
     rank = lax.axis_index("blk")
     me = lax.axis_index("fsdp")
@@ -61,7 +60,7 @@
     model = part * group
     scale = 1.0 / math.sqrt(width)
     rate = 0.5 * math.sqrt(width / (per * group))
-    piece = width // CHUNKS
+    step = width // CUTS[-1]
 
     def peer(i):
         return lax.rem(me + i, group)
@@ -77,7 +76,7 @@
     pl.semaphore_wait(barrier, group + 1)
 
     def weight_copy(way, c):
-        rows = pl.ds(c * piece, piece)
+        rows = pl.ds(CUTS[c] * step, (CUTS[c + 1] - CUTS[c]) * step)
         other, landing = ((up, low), (down, high))[way]
         return pltpu.make_async_remote_copy(
             src_ref=weight.at[rows],
@@ -228,21 +227,6 @@
         )
         acc[rows, :] = own_c * own[rows, :].astype(jnp.float32) - (rate * scale) * grad
 
-    def result(c):
-        rows = pl.ds(c * piece, piece)
-        return pltpu.make_async_copy(stage.at[rows], out.at[rows], o_sem.at[c])
-
-    for c in range(CHUNKS):
-        rows = pl.ds(c * piece, piece)
-        for way in range(2):
-            weight_copy(way, c).wait_recv()
-        stage[rows, :] = (
-            acc[rows, :]
-            + low_c * low[rows, :].astype(jnp.float32)
-            + high_c * high[rows, :].astype(jnp.float32)
-        ).astype(jnp.bfloat16)
-        result(c).start()
-
     for i in range(1, group):
         p = peer(i)
         token_copy(context, me, p).wait_send()
@@ -250,10 +234,20 @@
         grad_copy(me, p).wait_send()
     for way in range(2):
         count_copy(way).wait_send()
+
+    for c in range(CHUNKS):
+        rows = pl.ds(CUTS[c] * step, (CUTS[c + 1] - CUTS[c]) * step)
+        for way in range(2):
+            weight_copy(way, c).wait_recv()
+        out[rows, :] = (
+            acc[rows, :]
+            + low_c * low[rows, :].astype(jnp.float32)
+            + high_c * high[rows, :].astype(jnp.float32)
+        ).astype(jnp.bfloat16)
+
+    for way in range(2):
         for c in range(CHUNKS):
             weight_copy(way, c).wait_send()
-    for c in range(CHUNKS):
-        result(c).wait()
 
 
 def body(context, hidden, cotangent, gain, weight, step_counts):
@@ -268,13 +262,12 @@
         functools.partial(kernel, blocks, group),
         out_shape=jax.ShapeDtypeStruct((width, part), half),
         in_specs=[hbm] * 5 + [pl.BlockSpec(memory_space=pltpu.SMEM)],
-        out_specs=pl.BlockSpec(memory_space=pl.ANY),
+        out_specs=pl.BlockSpec(memory_space=pltpu.VMEM),
         scratch_shapes=[
             pltpu.VMEM((width, part), half),
             pltpu.VMEM((width, part), half),
             pltpu.VMEM((width, part), half),
             pltpu.VMEM((width, part), jnp.float32),
-            pltpu.VMEM((width, part), half),
             pltpu.VMEM((per * group, width), half),
             pltpu.VMEM((per * group, part), half),
             pltpu.VMEM((per * group, part), half),
@@ -295,7 +288,6 @@
             pltpu.SemaphoreType.DMA((2,)),
             pltpu.SemaphoreType.DMA((2,)),
             pltpu.SemaphoreType.DMA((6,)),
-            pltpu.SemaphoreType.DMA((CHUNKS,)),
         ],
         compiler_params=pltpu.CompilerParams(
             collective_id=1, has_side_effects=True, vmem_limit_bytes=46 * 2**20

time: 101 us -> 101 us (level)
  no operation moved by 1% of the time
where the time goes in v3:
time: 101 us; the launch traced here: 100 us
  Pallas kernels  97.7 us (97%)
  local copies, waits for them, and re-layouts  2.02 us (2%)
    pallas_call x1, Pallas kernels, body(): pl.pallas_call(functools.partial(kernel, blocks, group), out_shape=jax.Sh...  97.7 us

profile of v3, /device:TPU:0, one launch (start us, length us, event | category | flops | bytes accessed | tf_op | source)
XLA Modules:
  0.0 100.4 jit_solution(386254908809598552)
XLA Ops:
  0.7 97.7 %shard_map.64 = bf16[2048,1024]{1,0:T(8,128)(2,1)S(1)} custom-call(bf16[128,2048]{1,0:T(8,128)(2,1)} %bitcast.9, bf16[128,4096]{1,0:T(8,128)(2,1)} %bitcast.7, bf16[128,4096]{1,0:T(8,128)(2,1)} %bitcast.8, f32[1,4096]{1,0:T(1,128)} %gain.1, bf16[2048,1024]{1,0:T(8,128)(2,1)} %bitcast.6, s32[1]{0:T(128)S(6)} %copy.8.count), custom_call_target="tpu_custom_call" | custom-call | flops 4294967296 | bytes 25165824 | tf_op jit(solution)/shard_map/pallas_call | solution.py:261
  98.4 2.0 %copy.9 = bf16[1,2048,1024]{2,1,0:T(8,128)(2,1)} copy(bf16[1,2048,1024]{2,1,0:T(8,128)(2,1)S(1)} %bitcast.5) | data formatting | bytes 8388608
